TPU v7x, 128 devices: a whole 4x4x4 slice. The times are simulated.
128 devices in a mesh: rep: 16 (over y_lo, x, core), dp: 8 (over y_hi, z).
Axes of the slice: x: 4, y: 4 (y_hi: 2, y_lo: 2; y = y_hi * 2 + y_lo), z: 4, core: 2. Of those that a mesh axis runs over, the one named last changes fastest.
Arguments:
- queries: bfloat16 [2048, 64, 576], P(('rep', 'dp')), parts along dimension 0, may hold values from -50 to 50
- latent_cache: bfloat16 [2048, 512, 576], P(('rep', 'dp')), parts along dimension 0, may hold values from -8 to 8
- new_latent: bfloat16 [2048, 576], P(('rep', 'dp')), parts along dimension 0, may hold values from -6 to 6
- lengths: int32 [2048], P('rep'), parts along dimension 0, may hold values from 2 to 512, as said below
- value_up: bfloat16 [64, 512, 128], P('dp'), may hold values from -0.75 to 0.75
- output_proj: bfloat16 [8192, 7168], P('dp'), may hold values from -0.0625 to 0.0625
- residual: bfloat16 [2048, 7168], P(('rep', 'dp')), parts along dimension 0, may hold values from -3 to 3
- norm_gain: bfloat16 [7168], replicated, may hold values from 0.5 to 1.5
Outputs:
- hidden_next: bfloat16 [2048, 7168], P(('rep', 'dp')), parts along dimension 0
- normed: bfloat16 [2048, 7168], P(('rep', 'dp')), parts along dimension 0
There are 16 independent parts, one for each index of `rep`. A program takes and returns all parts, laid end to end along the dimension named above; an argument that names none is the same for every part. Nothing has to cross between parts.
Inputs may be any that keep to these rules, and one draw needn't show every extreme that they name: The rows of one device share a ceiling of 128, 256 or 512 on their lengths; one device of each part has the ceiling 512 and a row of exactly 512.
All inputs are finite; a program needn't handle non-finite values.
Results may differ from a plain program's by a relative error of at most 0.017.
Values may be sent and summed in bfloat16 or wider, within the bound.
No kernel may reach another device: no remote copies, remote signals or barrier semaphores. Data moves between devices by JAX's collectives and lax.ppermute only.
A program may use at most 128 MiB of HBM per device.

v0:
```python
import jax
import jax.numpy as jnp
from jax import lax
from jax.sharding import PartitionSpec as P

LAT = 512
BLOCK = 256


score_scale = 192.0 ** (-0.5)
norm_eps = 1e-06


def over_blocks(block_counts, block_step, running):

    def outer(group_index, running):
        return lax.fori_loop(
            0,
            block_counts[group_index],
            lambda block_index, inner_running: block_step(group_index, block_index, inner_running),
            running,
        )

    return lax.fori_loop(0, block_counts.shape[0], outer, running)


def attend(queries, latent_cache, new_latent, lengths_here, group_count):
    row_count, span, width = latent_cache.shape
    heads = queries.shape[1]
    group_rows = row_count // group_count
    block_size = min(BLOCK, span)
    group_longest = jnp.max(lengths_here.reshape(group_count, group_rows), axis=1)
    block_counts = (group_longest + block_size - 1) // block_size

    def score_step(group_index, block_index, buffer):
        row_start = group_index * group_rows
        cache_tile = lax.dynamic_slice(
            latent_cache, (row_start, block_index * block_size, 0), (group_rows, block_size, width)
        )
        queries_tile = lax.dynamic_slice_in_dim(queries, row_start, group_rows, 0)
        tile_scores = (
            jnp.einsum("rhk,rpk->rhp", queries_tile, cache_tile, preferred_element_type=jnp.float32)
            * score_scale
        )
        return lax.dynamic_update_slice(
            buffer, tile_scores, (row_start, 0, block_index * block_size)
        )

    scores = over_blocks(block_counts, score_step, jnp.zeros((row_count, heads, span), jnp.float32))
    self_score = (
        jnp.einsum("rhk,rk->rh", queries, new_latent, preferred_element_type=jnp.float32)
        * score_scale
    )
    visible = jnp.arange(span)[None, None, :] < lengths_here[:, None, None]
    scores = jnp.where(visible, scores, -jnp.inf)
    row_max = jnp.maximum(jnp.max(scores, axis=2), self_score)
    raised = jnp.exp(scores - row_max[:, :, None])
    self_raised = jnp.exp(self_score - row_max)
    row_total = jnp.sum(raised, axis=2) + self_raised
    weights = raised.astype(jnp.bfloat16)
    self_weight = lax.optimization_barrier(self_raised.astype(jnp.bfloat16)).astype(jnp.float32)
    start_sum = self_weight[:, :, None] * new_latent[:, None, :LAT].astype(jnp.float32)

    def value_step(group_index, block_index, gathered):
        row_start = group_index * group_rows
        cache_tile = lax.dynamic_slice(
            latent_cache, (row_start, block_index * block_size, 0), (group_rows, block_size, LAT)
        )
        weight_tile = lax.dynamic_slice(
            weights, (row_start, 0, block_index * block_size), (group_rows, heads, block_size)
        )
        current = lax.dynamic_slice_in_dim(gathered, row_start, group_rows, 0)
        current = current + jnp.einsum(
            "rhp,rpc->rhc", weight_tile, cache_tile, preferred_element_type=jnp.float32
        )
        return lax.dynamic_update_slice_in_dim(gathered, current, row_start, 0)

    gathered = over_blocks(block_counts, value_step, start_sum)
    return (gathered / row_total[:, :, None]).astype(jnp.bfloat16)


def per_device(
    queries, latent_cache, new_latent, lengths, value_up, output_proj, residual, norm_gain
):
    group_count = lax.axis_size("dp")
    rank_here = lax.axis_index("dp")
    rows_here = latent_cache.shape[0]
    queries_here, cache_here, latent_here = (queries, latent_cache, new_latent)
    lengths_here = lax.dynamic_slice_in_dim(lengths, rank_here * rows_here, rows_here)
    latent_out = attend(queries_here, cache_here, latent_here, lengths_here, group_count)
    heads_here = value_up.shape[0]
    owned_latent = lax.all_to_all(latent_out, "dp", split_axis=1, concat_axis=0, tiled=True)
    owned_values = jnp.einsum(
        "rhc,hcv->rhv", owned_latent, value_up, preferred_element_type=jnp.float32
    ).astype(jnp.bfloat16)
    flattened = owned_values.reshape(group_count * rows_here, heads_here * owned_values.shape[2])
    attention = lax.psum_scatter(
        jnp.dot(flattened, output_proj, preferred_element_type=jnp.float32).astype(jnp.bfloat16),
        "dp",
        scatter_dimension=0,
        tiled=True,
    ).astype(jnp.float32)
    summed = residual.astype(jnp.float32) + attention
    hidden_next = summed.astype(jnp.bfloat16)
    inverse_rms = lax.rsqrt(jnp.mean(summed * summed, axis=1, keepdims=True) + norm_eps)
    normed = (summed * inverse_rms * norm_gain.astype(jnp.float32)).astype(jnp.bfloat16)
    return (hidden_next, normed)


def solution(mesh):
    return jax.shard_map(
        per_device,
        mesh=mesh,
        in_specs=(
            P(("rep", "dp"), None, None),
            P(("rep", "dp"), None, None),
            P(("rep", "dp"), None),
            P("rep"),
            P("dp", None, None),
            P("dp", None),
            P(("rep", "dp"), None),
            P(),
        ),
        out_specs=(P(("rep", "dp"), None), P(("rep", "dp"), None)),
        check_vma=False,
    )
```

profile of v0, /device:TPU:0, one launch (start us, length us, event | category | flops | bytes accessed | tf_op | source)
XLA Modules:
  0.0 227.0 jit_solution(14718094092691013660)
XLA Ops:
  7.2 0.8 dynamic_slice.42
  8.3 14.1 %copy.22 = bf16[16,512,576]{2,1,0:T(8,128)(2,1)} copy(bf16[16,512,576]{1,2,0:T(8,128)(2,1)} %param.17) | data formatting | bytes 18874368 | tf_op jit(solution)/shard_map/while | solution.py:24
  22.7 34.3 %while.71 = (s32[]{:T(128)}, f32[16,64,512]{2,1,0:T(8,128)S(1)}, s32[8]{0:T(128)S(1)}, bf16[16,64,576]{2,1,0:T(8,128)(2,1)}, bf16[16,512,576]{1,2,0:T(8,128)(2,1...) while((s32[]{:T(128)}, f32[16,64,512]{2,1,0:T(8,128)S(1)}, ...), condition=%wide.region_4.5_spmd, body=%wide.region_1.4_spmd.sunk | while | flops 37781512 | bytes 1182118 | solution.py:24
  22.8 0.9 constant_dynamic-slice_fusion.2
  23.7 0.7 dynamic_slice.59
  24.3 2.7 %while.74 = (s32[]{:T(128)}, f32[16,64,512]{2,1,0:T(8,128)S(1)}, s32[]{:T(128)}, bf16[16,512,576]{1,2,0:T(8,128)(2,1)}, s32[]{:T(128)}, /*index=5*/bf16[2,64,576...) while((s32[]{:T(128)}, f32[16,64,512]{2,1,0:T(8,128)S(1)}, s32[]{:T(128)}, ...), condition=%wide.region_3.3_spmd, body=%wide.region_2.2_spmd.sunk | while | flops 37781508 | bytes 886931 | solution.py:17
  25.0 1.3 fusion.33
  27.0 0.9 constant_dynamic-slice_fusion.2
  28.0 0.7 dynamic_slice.59
  28.6 2.7 %while.74 = (s32[]{:T(128)}, f32[16,64,512]{2,1,0:T(8,128)S(1)}, s32[]{:T(128)}, bf16[16,512,576]{1,2,0:T(8,128)(2,1)}, s32[]{:T(128)}, /*index=5*/bf16[2,64,576...) while((s32[]{:T(128)}, f32[16,64,512]{2,1,0:T(8,128)S(1)}, s32[]{:T(128)}, ...), condition=%wide.region_3.3_spmd, body=%wide.region_2.2_spmd.sunk | while | flops 37781508 | bytes 886931 | solution.py:17
  29.3 1.3 fusion.33
  31.3 0.9 constant_dynamic-slice_fusion.2
  32.3 0.7 dynamic_slice.59
  32.9 2.7 %while.74 = (s32[]{:T(128)}, f32[16,64,512]{2,1,0:T(8,128)S(1)}, s32[]{:T(128)}, bf16[16,512,576]{1,2,0:T(8,128)(2,1)}, s32[]{:T(128)}, /*index=5*/bf16[2,64,576...) while((s32[]{:T(128)}, f32[16,64,512]{2,1,0:T(8,128)S(1)}, s32[]{:T(128)}, ...), condition=%wide.region_3.3_spmd, body=%wide.region_2.2_spmd.sunk | while | flops 37781508 | bytes 886931 | solution.py:17
  33.6 1.3 fusion.33
  35.6 0.9 constant_dynamic-slice_fusion.2
  36.6 0.7 dynamic_slice.59
  37.2 2.7 %while.74 = (s32[]{:T(128)}, f32[16,64,512]{2,1,0:T(8,128)S(1)}, s32[]{:T(128)}, bf16[16,512,576]{1,2,0:T(8,128)(2,1)}, s32[]{:T(128)}, /*index=5*/bf16[2,64,576...) while((s32[]{:T(128)}, f32[16,64,512]{2,1,0:T(8,128)S(1)}, s32[]{:T(128)}, ...), condition=%wide.region_3.3_spmd, body=%wide.region_2.2_spmd.sunk | while | flops 37781508 | bytes 886931 | solution.py:17
  37.9 1.3 fusion.33
  39.9 0.9 constant_dynamic-slice_fusion.2
  40.8 0.7 dynamic_slice.59
  41.5 2.7 %while.74 = (s32[]{:T(128)}, f32[16,64,512]{2,1,0:T(8,128)S(1)}, s32[]{:T(128)}, bf16[16,512,576]{1,2,0:T(8,128)(2,1)}, s32[]{:T(128)}, /*index=5*/bf16[2,64,576...) while((s32[]{:T(128)}, f32[16,64,512]{2,1,0:T(8,128)S(1)}, s32[]{:T(128)}, ...), condition=%wide.region_3.3_spmd, body=%wide.region_2.2_spmd.sunk | while | flops 37781508 | bytes 886931 | solution.py:17
  42.2 1.3 fusion.33
  44.2 0.9 constant_dynamic-slice_fusion.2
  45.1 0.7 dynamic_slice.59
  45.8 2.7 %while.74 = (s32[]{:T(128)}, f32[16,64,512]{2,1,0:T(8,128)S(1)}, s32[]{:T(128)}, bf16[16,512,576]{1,2,0:T(8,128)(2,1)}, s32[]{:T(128)}, /*index=5*/bf16[2,64,576...) while((s32[]{:T(128)}, f32[16,64,512]{2,1,0:T(8,128)S(1)}, s32[]{:T(128)}, ...), condition=%wide.region_3.3_spmd, body=%wide.region_2.2_spmd.sunk | while | flops 37781508 | bytes 886931 | solution.py:17
  46.5 1.3 fusion.33
  48.5 0.9 constant_dynamic-slice_fusion.2
  49.4 0.7 dynamic_slice.59
  50.1 2.7 %while.74 = (s32[]{:T(128)}, f32[16,64,512]{2,1,0:T(8,128)S(1)}, s32[]{:T(128)}, bf16[16,512,576]{1,2,0:T(8,128)(2,1)}, s32[]{:T(128)}, /*index=5*/bf16[2,64,576...) while((s32[]{:T(128)}, f32[16,64,512]{2,1,0:T(8,128)S(1)}, s32[]{:T(128)}, ...), condition=%wide.region_3.3_spmd, body=%wide.region_2.2_spmd.sunk | while | flops 37781508 | bytes 886931 | solution.py:17
  50.8 1.3 fusion.33
  52.8 0.9 constant_dynamic-slice_fusion.2
  53.7 0.7 dynamic_slice.59
  54.3 2.7 %while.74 = (s32[]{:T(128)}, f32[16,64,512]{2,1,0:T(8,128)S(1)}, s32[]{:T(128)}, bf16[16,512,576]{1,2,0:T(8,128)(2,1)}, s32[]{:T(128)}, /*index=5*/bf16[2,64,576...) while((s32[]{:T(128)}, f32[16,64,512]{2,1,0:T(8,128)S(1)}, s32[]{:T(128)}, ...), condition=%wide.region_3.3_spmd, body=%wide.region_2.2_spmd.sunk | while | flops 37781508 | bytes 886931 | solution.py:17
  55.0 1.3 fusion.33
  57.1 1.8 fusion.12
  59.1 1.5 fusion.9
  60.9 25.5 %while.73 = (s32[]{:T(128)}, f32[16,64,512]{2,1,0:T(8,128)S(1)}, s32[8]{0:T(128)S(1)}, bf16[16,64,512]{2,1,0:T(8,128)(2,1)}, bf16[16,512,576]{2,1,0:T(8,128)(2,1...) while((s32[]{:T(128)}, f32[16,64,512]{2,1,0:T(8,128)S(1)}, ...), condition=%wide.region_9.10_spmd, body=%wide.region_6.9_spmd.sunk | while | flops 33619976 | bytes 1117090 | solution.py:24
  60.9 0.6 dynamic_slice.60
  61.5 2.5 %while.75 = (s32[]{:T(128)}, f32[16,64,512]{2,1,0:T(8,128)S(1)}, s32[]{:T(128)}, s32[]{:T(128)}, bf16[16,64,512]{2,1,0:T(8,128)(2,1)}, /*index=5*/bf16[16,512,57...) while((s32[]{:T(128)}, f32[16,64,512]{2,1,0:T(8,128)S(1)}, s32[]{:T(128)}, s32[]{:T(128)}, ...), condition=%wide.region_8.8_spmd, body=%wide.region_7.7_spmd.sunk | while | flops 33619972 | bytes 1116819 | solution.py:17
  62.1 1.3 fusion.30
  64.1 0.6 dynamic_slice.60
  64.7 2.5 %while.75 = (s32[]{:T(128)}, f32[16,64,512]{2,1,0:T(8,128)S(1)}, s32[]{:T(128)}, s32[]{:T(128)}, bf16[16,64,512]{2,1,0:T(8,128)(2,1)}, /*index=5*/bf16[16,512,57...) while((s32[]{:T(128)}, f32[16,64,512]{2,1,0:T(8,128)S(1)}, s32[]{:T(128)}, s32[]{:T(128)}, ...), condition=%wide.region_8.8_spmd, body=%wide.region_7.7_spmd.sunk | while | flops 33619972 | bytes 1116819 | solution.py:17
  65.3 1.3 fusion.30
  67.3 0.6 dynamic_slice.60
  67.9 2.5 %while.75 = (s32[]{:T(128)}, f32[16,64,512]{2,1,0:T(8,128)S(1)}, s32[]{:T(128)}, s32[]{:T(128)}, bf16[16,64,512]{2,1,0:T(8,128)(2,1)}, /*index=5*/bf16[16,512,57...) while((s32[]{:T(128)}, f32[16,64,512]{2,1,0:T(8,128)S(1)}, s32[]{:T(128)}, s32[]{:T(128)}, ...), condition=%wide.region_8.8_spmd, body=%wide.region_7.7_spmd.sunk | while | flops 33619972 | bytes 1116819 | solution.py:17
  68.5 1.3 fusion.30
  70.4 0.6 dynamic_slice.60
  71.1 2.5 %while.75 = (s32[]{:T(128)}, f32[16,64,512]{2,1,0:T(8,128)S(1)}, s32[]{:T(128)}, s32[]{:T(128)}, bf16[16,64,512]{2,1,0:T(8,128)(2,1)}, /*index=5*/bf16[16,512,57...) while((s32[]{:T(128)}, f32[16,64,512]{2,1,0:T(8,128)S(1)}, s32[]{:T(128)}, s32[]{:T(128)}, ...), condition=%wide.region_8.8_spmd, body=%wide.region_7.7_spmd.sunk | while | flops 33619972 | bytes 1116819 | solution.py:17
  71.7 1.3 fusion.30
  74.2 2.5 %while.75 = (s32[]{:T(128)}, f32[16,64,512]{2,1,0:T(8,128)S(1)}, s32[]{:T(128)}, s32[]{:T(128)}, bf16[16,64,512]{2,1,0:T(8,128)(2,1)}, /*index=5*/bf16[16,512,57...) while((s32[]{:T(128)}, f32[16,64,512]{2,1,0:T(8,128)S(1)}, s32[]{:T(128)}, s32[]{:T(128)}, ...), condition=%wide.region_8.8_spmd, body=%wide.region_7.7_spmd.sunk | while | flops 33619972 | bytes 1116819 | solution.py:17
  74.9 1.3 fusion.30
  77.4 2.5 %while.75 = (s32[]{:T(128)}, f32[16,64,512]{2,1,0:T(8,128)S(1)}, s32[]{:T(128)}, s32[]{:T(128)}, bf16[16,64,512]{2,1,0:T(8,128)(2,1)}, /*index=5*/bf16[16,512,57...) while((s32[]{:T(128)}, f32[16,64,512]{2,1,0:T(8,128)S(1)}, s32[]{:T(128)}, s32[]{:T(128)}, ...), condition=%wide.region_8.8_spmd, body=%wide.region_7.7_spmd.sunk | while | flops 33619972 | bytes 1116819 | solution.py:17
  78.1 1.3 fusion.30
  80.6 2.5 %while.75 = (s32[]{:T(128)}, f32[16,64,512]{2,1,0:T(8,128)S(1)}, s32[]{:T(128)}, s32[]{:T(128)}, bf16[16,64,512]{2,1,0:T(8,128)(2,1)}, /*index=5*/bf16[16,512,57...) while((s32[]{:T(128)}, f32[16,64,512]{2,1,0:T(8,128)S(1)}, s32[]{:T(128)}, s32[]{:T(128)}, ...), condition=%wide.region_8.8_spmd, body=%wide.region_7.7_spmd.sunk | while | flops 33619972 | bytes 1116819 | solution.py:17
  81.2 1.3 fusion.30
  83.8 2.5 %while.75 = (s32[]{:T(128)}, f32[16,64,512]{2,1,0:T(8,128)S(1)}, s32[]{:T(128)}, s32[]{:T(128)}, bf16[16,64,512]{2,1,0:T(8,128)(2,1)}, /*index=5*/bf16[16,512,57...) while((s32[]{:T(128)}, f32[16,64,512]{2,1,0:T(8,128)S(1)}, s32[]{:T(128)}, s32[]{:T(128)}, ...), condition=%wide.region_8.8_spmd, body=%wide.region_7.7_spmd.sunk | while | flops 33619972 | bytes 1116819 | solution.py:17
  84.4 1.3 fusion.30
  86.5 1.2 fusion.8
  87.7 48.6 %all_to_all.18 = bf16[16,64,512]{2,0,1:T(8,128)(2,1)S(1)} all-to-all(bf16[16,64,512]{2,0,1:T(8,128)(2,1)S(1)} %fusion.8), channel_id=1, replica_groups=mesh['rep'=16,'dp'=8] {'dp'}, dimensions={1} | all-to-all | bytes 2097152 | tf_op jit(solution)/shard_map/all_to_all | solution.py:92
  136.9 8.7 %convolution_convert_fusion = bf16[128,7168]{1,0:T(8,128)(2,1)} fusion(bf16[128,1024]{0,1:T(8,128)(2,1)S(1)} %bitcast.32, bf16[1024,7168]{1,0:T(8,128)(2,1)} %param.21), kind=kOutput, calls=%fused_computation.11 | convolution fusion | flops 1879965696 | bytes 16777216 | tf_op jit(solution)/shard_map/dot_general | solution.py:98
  145.6 71.6 %reduce-scatter.2.cloned.1.call-done = bf16[16,7168]{1,0:T(8,128)(2,1)} async-done(((bf16[128,7168]{1,0:T(8,128)(2,1)}), bf16[16,7168]{1,0:T(8,128)(2,1)}) %reduce-scatter.2.cloned.1.call-update) | async-done | bytes 229392 | tf_op jit(solution)/shard_map/reduce_scatter | solution.py:97
  217.2 1.1 multiply_reduce_fusion
  218.3 1.8 multiply_convert_fusion
  (30 shorter events, 4.2 us)
Async XLA Ops:
  7.2 129.2 %copy-start = (bf16[8,512,128]{2,1,0:T(8,128)(2,1)S(1)}, bf16[8,512,128]{2,1,0:T(8,128)(2,1)}, u32[]{:S(2)}) copy-start(bf16[8,512,128]{2,1,0:T(8,128)(2,1)} %param.20) | copy-start | bytes 3145732
  7.2 210.0 %reduce-scatter.2.cloned.1.call-start = ((), (), s32[]{:S(2)}) async-start(), calls=%async_computation.2 | async-start | bytes 2064384 | tf_op jit(solution)/shard_map/reduce_scatter | solution.py:97
  22.7 34.3 %copy-start.3 = (bf16[16,576]{1,0:T(8,128)(2,1)S(1)}, bf16[16,576]{1,0:T(8,128)(2,1)}, u32[]{:S(2)}) copy-start(bf16[16,576]{1,0:T(8,128)(2,1)} %param.18) | copy-start | bytes 55300
  136.8 8.7 %copy-start.2 = (bf16[7168]{0:T(1024)(128)(2,1)S(1)}, bf16[7168]{0:T(1024)(128)(2,1)}, u32[]{:S(2)}) copy-start(bf16[7168]{0:T(1024)(128)(2,1)} %param.23) | copy-start | bytes 43012
  136.9 80.4 %copy-start.1 = (bf16[16,7168]{1,0:T(8,128)(2,1)S(1)}, bf16[16,7168]{1,0:T(8,128)(2,1)}, u32[]{:S(2)}) copy-start(bf16[16,7168]{1,0:T(8,128)(2,1)} %param.22) | copy-start | bytes 688132
Sparse Core Ops, SparseCore 0:
  145.7 71.4 reduce-scatter.1
where the time goes:
time: 229 us; the launch traced here: 227 us
  waiting for transfers between devices  71.6 us (31%)
  blocking collectives  48.6 us (21%)
  local copies, waits for them, and re-layouts  33.1 us (14%)
  matrix products  31.8 us (14%)
  loops' own time  21.3 us (9%)
  between operations  14.2 us (6%)
  other arithmetic  6.27 us (3%)
    reduce_scatter x1, waiting for transfers between devices, per_device(): lax.psum_scatter(jnp.dot(flattened, output_proj, preferred_element_type=j...  71.6 us
    all_to_all x1, blocking collectives, per_device(): lax.all_to_all(latent_out, 'dp', split_axis=1, concat_axis=0, tiled=True)  48.6 us
    another operation x16, loops' own time, outer(): lax.fori_loop(0, block_counts[group_index], lambda block_index, inner_run...  20.9 us
    while x1, local copies, waits for them, and re-layouts, over_blocks(): return lax.fori_loop(0, block_counts.shape[0], outer, running)  14.1 us
    dot_general x8, matrix products, score_step(): jnp.einsum('rhk,rpk->rhp', queries_tile, cache_tile, preferred_element_ty...  10.4 us
    dot_general x8, matrix products, value_step(): jnp.einsum('rhp,rpc->rhc', weight_tile, cache_tile, preferred_element_typ...  10.4 us
    dynamic_slice x16, local copies, waits for them, and re-layouts, outer(): block_counts[group_index]  10.1 us
    dot_general x1, matrix products, per_device(): jnp.dot(flattened, output_proj, preferred_element_type=jnp.float32)  8.66 us
  transfers between devices with their start and end apart: 1, of which 1 were waited for; matrix products, arithmetic and copies ran while one was open for 0% of the time, Pallas kernels for 0%

commit v1 on v0

v1 whole, which is shorter than its diff:
```python
import jax
import jax.numpy as jnp
from jax import lax
from jax.experimental import pallas as pl
from jax.experimental.pallas import tpu as pltpu
from jax.sharding import PartitionSpec as P

LAT = 512
SPAN_STEP = 128
GROUP_ROWS = 2
score_scale = 192.0 ** (-0.5)
norm_eps = 1e-06
MIB = 1024 * 1024


def attend_kernel(lengths_ref, queries_ref, latent_ref, cache_ref, out_ref, held, latent_wide, arrived):
    row_count, span, width = held.shape
    heads = queries_ref.shape[1]
    group_count = row_count // GROUP_ROWS
    levels = span // SPAN_STEP

    def group_level(group):
        longest = lengths_ref[group * GROUP_ROWS]
        for i in range(1, GROUP_ROWS):
            longest = jnp.maximum(longest, lengths_ref[group * GROUP_ROWS + i])
        return (longest + SPAN_STEP - 1) // SPAN_STEP

    def fetch(group, level):
        rows = pl.ds(group * GROUP_ROWS, GROUP_ROWS)
        keys = pl.ds(0, level * SPAN_STEP)
        return pltpu.make_async_copy(
            cache_ref.at[rows, keys, :], held.at[rows, keys, :], arrived.at[group]
        )

    def start(group, carry):
        here = group_level(group)
        for level in range(1, levels + 1):

            @pl.when(here == level)
            def _():
                fetch(group, level).start()

        return carry

    lax.fori_loop(0, group_count, start, 0)
    latent_wide[...] = latent_ref[...].astype(jnp.float32)

    def attend_row(row, level):
        length = lengths_ref[row]
        queries = queries_ref[row]
        keys = held[row, : level * SPAN_STEP, :]
        fresh = latent_wide[pl.ds(row, 1), :]
        scores = (
            lax.dot_general(
                queries, keys, (((1,), (1,)), ((), ())), preferred_element_type=jnp.float32
            )
            * score_scale
        )
        self_score = (
            jnp.sum(queries.astype(jnp.float32) * fresh, axis=1, keepdims=True) * score_scale
        )
        position = lax.broadcasted_iota(jnp.int32, scores.shape, 1)
        scores = jnp.where(position < length, scores, -jnp.inf)
        row_max = jnp.maximum(jnp.max(scores, axis=1, keepdims=True), self_score)
        raised = jnp.exp(scores - row_max)
        self_raised = jnp.exp(self_score - row_max)
        row_total = jnp.sum(raised, axis=1, keepdims=True) + self_raised
        gathered = jnp.dot(
            raised.astype(jnp.bfloat16), keys[:, :LAT], preferred_element_type=jnp.float32
        )
        self_weight = self_raised.astype(jnp.bfloat16).astype(jnp.float32)
        gathered = gathered + self_weight * fresh[:, :LAT]
        return gathered / row_total

    def attend_group(group, carry):
        here = group_level(group)
        owners, rows_heads, _ = out_ref.shape
        owned = heads // owners
        for level in range(1, levels + 1):

            @pl.when(here == level)
            def _():
                fetch(group, level).wait()
                done = [
                    attend_row(group * GROUP_ROWS + i, level).reshape(owners, owned, LAT)
                    for i in range(GROUP_ROWS)
                ]
                block = jnp.concatenate(done, axis=1).astype(jnp.bfloat16)
                size = GROUP_ROWS * owned
                out_ref[:, pl.ds(pl.multiple_of(group * size, size), size), :] = block

        return carry

    lax.fori_loop(0, group_count, attend_group, 0)


def attend(queries, latent_cache, new_latent, lengths_here, owners):
    row_count, span, width = latent_cache.shape
    heads = queries.shape[1]
    owned = heads // owners
    vmem = pl.BlockSpec(memory_space=pltpu.VMEM)
    return pl.pallas_call(
        attend_kernel,
        out_shape=jax.ShapeDtypeStruct((owners, row_count * owned, LAT), jnp.bfloat16),
        in_specs=[
            pl.BlockSpec(memory_space=pltpu.SMEM),
            vmem,
            vmem,
            pl.BlockSpec(memory_space=pl.ANY),
        ],
        out_specs=vmem,
        scratch_shapes=[
            pltpu.VMEM((row_count, span, width), jnp.bfloat16),
            pltpu.VMEM((row_count, width), jnp.float32),
            pltpu.SemaphoreType.DMA((row_count // GROUP_ROWS,)),
        ],
        compiler_params=pltpu.CompilerParams(vmem_limit_bytes=32 * MIB),
        name="attend",
    )(lengths_here, queries, new_latent, latent_cache)


def project_kernel(latent_ref, value_up_ref, proj_ref, out_ref, wide, values):
    owned, lat, value_size = value_up_ref.shape
    rows = values.shape[0]

    @pl.when(pl.program_id(0) == 0)
    def _():
        for c in range(lat // 128):
            wide[c] = latent_ref[:, c * 128 : (c + 1) * 128].astype(jnp.float32)
        for h in range(owned):
            mine = jnp.concatenate(
                [wide[c, pl.ds(h, rows, stride=owned), :] for c in range(lat // 128)], axis=1
            ).astype(jnp.bfloat16)
            values[:, h * value_size : (h + 1) * value_size] = jnp.dot(
                mine, value_up_ref[h], preferred_element_type=jnp.float32
            ).astype(jnp.bfloat16)

    out_ref[...] = jnp.dot(
        values[...], proj_ref[...], preferred_element_type=jnp.float32
    ).astype(jnp.bfloat16)


def project(owned_latent, value_up, output_proj, rows):
    owned, lat, value_size = value_up.shape
    depth, width = output_proj.shape
    step = 1024
    return pl.pallas_call(
        project_kernel,
        grid=(width // step,),
        out_shape=jax.ShapeDtypeStruct((rows, width), jnp.bfloat16),
        in_specs=[
            pl.BlockSpec((rows * owned, lat), lambda i: (0, 0)),
            pl.BlockSpec((owned, lat, value_size), lambda i: (0, 0, 0)),
            pl.BlockSpec((depth, step), lambda i: (0, i)),
        ],
        out_specs=pl.BlockSpec((rows, step), lambda i: (0, i)),
        scratch_shapes=[
            pltpu.VMEM((lat // 128, rows * owned, 128), jnp.float32),
            pltpu.VMEM((rows, owned * value_size), jnp.bfloat16),
        ],
        compiler_params=pltpu.CompilerParams(vmem_limit_bytes=32 * MIB),
        name="project",
    )(owned_latent, value_up, output_proj)


def finish_kernel(partial_ref, residual_ref, gain_ref, hidden_ref, normed_ref):
    summed = residual_ref[...].astype(jnp.float32)
    for g in range(partial_ref.shape[0]):
        summed = summed + partial_ref[g].astype(jnp.float32)
    hidden_ref[...] = summed.astype(jnp.bfloat16)
    mean = jnp.mean(summed * summed, axis=1, keepdims=True)
    normed = summed * lax.rsqrt(mean + norm_eps) * gain_ref[...].astype(jnp.float32)
    normed_ref[...] = normed.astype(jnp.bfloat16)


def finish(partials, residual, norm_gain):
    vmem = pl.BlockSpec(memory_space=pltpu.VMEM)
    shape = jax.ShapeDtypeStruct(residual.shape, jnp.bfloat16)
    return pl.pallas_call(
        finish_kernel,
        out_shape=(shape, shape),
        in_specs=[vmem, vmem, vmem],
        out_specs=(vmem, vmem),
        compiler_params=pltpu.CompilerParams(vmem_limit_bytes=32 * MIB),
        name="finish",
    )(partials, residual, norm_gain.reshape(1, -1))


def per_device(
    queries, latent_cache, new_latent, lengths, value_up, output_proj, residual, norm_gain
):
    owners = lax.axis_size("dp")
    rank_here = lax.axis_index("dp")
    rows_here = latent_cache.shape[0]
    owned = value_up.shape[0]
    lengths_here = lax.dynamic_slice_in_dim(lengths, rank_here * rows_here, rows_here)
    latent_out = attend(queries, latent_cache, new_latent, lengths_here, owners)
    owned_latent = lax.all_to_all(latent_out, "dp", split_axis=0, concat_axis=0, tiled=True)
    rows = owners * rows_here
    partial = project(
        owned_latent.reshape(rows * owned, LAT), value_up, output_proj, rows
    )
    partials = lax.all_to_all(
        partial.reshape(owners, rows_here, -1), "dp", split_axis=0, concat_axis=0, tiled=True
    )
    return finish(partials, residual, norm_gain)


def solution(mesh):
    return jax.shard_map(
        per_device,
        mesh=mesh,
        in_specs=(
            P(("rep", "dp"), None, None),
            P(("rep", "dp"), None, None),
            P(("rep", "dp"), None),
            P("rep"),
            P("dp", None, None),
            P("dp", None),
            P(("rep", "dp"), None),
            P(),
        ),
        out_specs=(P(("rep", "dp"), None), P(("rep", "dp"), None)),
        check_vma=False,
    )
```

time: 229 us -> 93.3 us (0.41)
  the two profiles are of different devices: /device:TPU:0 before, /device:TPU:24 now
where the time goes in v1:
time: 93.3 us; the launch traced here: 92.1 us
  local copies, waits for them, and re-layouts  23.6 us (25%)
  blocking collectives  23.6 us (25%)
  waiting for transfers between devices  22.3 us (24%)
  Pallas kernels  15.7 us (17%)
  starting transfers between devices  6.28 us (7%)
    all_to_all x1, blocking collectives, per_device(): lax.all_to_all(latent_out, 'dp', split_axis=0, concat_axis=0, tiled=True)  23.6 us
    unnamed x17, local copies, waits for them, and re-layouts  23.5 us
    all_to_all x1, waiting for transfers between devices, per_device(): lax.all_to_all(partial.reshape(owners, rows_here, -1), 'dp', split_axis=0...  22.3 us
    pallas_call x1, Pallas kernels, attend(): pl.pallas_call(attend_kernel, out_shape=jax.ShapeDtypeStruct((owners, row...  8.49 us
    all_to_all x1, starting transfers between devices, per_device(): lax.all_to_all(partial.reshape(owners, rows_here, -1), 'dp', split_axis=0...  6.28 us
    pallas_call x1, Pallas kernels, project(): pl.pallas_call(project_kernel, grid=(width // step,), out_shape=jax.Shape...  6.01 us
  transfers between devices with their start and end apart: 1, of which 1 were waited for; matrix products, arithmetic and copies ran while one was open for 0% of the time, Pallas kernels for 0%

profile of v1, /device:TPU:24, one launch (start us, length us, event | category | flops | bytes accessed | tf_op | source)
XLA Modules:
  0.0 92.1 jit_solution(3726194524274170706)
XLA Ops:
  0.6 0.0 copy-start.7
  0.6 0.0 copy-start.2
  0.7 0.0 copy-start.5
  0.7 0.0 copy-start.3
  0.7 14.3 %copy.10.cache_ref = bf16[16,512,576]{2,1,0:T(8,128)(2,1)} copy(bf16[16,512,576]{1,2,0:T(8,128)(2,1)} %param.9) | data formatting | bytes 18874368 | tf_op args[1]
  15.0 0.0 copy-done.7
  15.0 0.1 dynamic_slice.3.lengths_ref
  15.0 0.0 copy-done.2
  15.0 0.0 copy-done.5
  15.0 0.0 copy-start
  15.0 4.0 %copy-done = bf16[16,512,576]{2,1,0:T(8,128)(2,1)S(1)} copy-done((bf16[16,512,576]{2,1,0:T(8,128)(2,1)S(1)}, bf16[16,512,576]{2,1,0:T(8,128)(2,1)}, u32[]{:S(2)}) %copy-start) | copy-done | bytes 9437208
  19.0 8.5 %attend.1 = bf16[8,128,512]{2,1,0:T(8,128)(2,1)S(1)} custom-call(s32[16]{0:T(128)S(1)} %dynamic_slice.3.lengths_ref, bf16[16,64,576]{2,1,0:T(8,128)(2,1)S(1)} %copy-done.2, bf16[16,576]{1,0:T(8,128)(2,1)S(1)} %copy-done.5, bf16[16,512,576]{2,1,0:T(8,128)(2,1)S(1)} %copy-done), custom_call_target="tpu_custom_call" | custom-call | tf_op jit(solution)/shard_map/attend/pallas_call | solution.py:102
  27.5 23.6 %all_to_all.10 = bf16[8,128,512]{2,1,0:T(8,128)(2,1)S(1)} all-to-all(bf16[8,128,512]{2,1,0:T(8,128)(2,1)S(1)} %attend.1), channel_id=1, replica_groups=mesh['rep'=16,'dp'=8] {'dp'}, dimensions={0} | all-to-all | bytes 2097152 | tf_op jit(solution)/shard_map/all_to_all | solution.py:198
  51.2 0.0 copy-done.3
  51.2 0.0 copy-start.1
  51.2 5.2 %copy-done.1 = bf16[1024,7168]{1,0:T(8,128)(2,1)S(1)} copy-done((bf16[1024,7168]{1,0:T(8,128)(2,1)S(1)}, bf16[1024,7168]{1,0:T(8,128)(2,1)}, u32[]{:S(2)}) %copy-start.1) | copy-done | bytes 14680088
  56.4 0.0 copy-start.6
  56.4 0.0 copy-start.4
  56.4 6.0 %project.1 = bf16[128,7168]{1,0:T(8,128)(2,1)} custom-call(bf16[1024,512]{1,0:T(8,128)(2,1)S(1)} %bitcast.2, bf16[8,512,128]{2,1,0:T(8,128)(2,1)S(1)} %copy-done.3, bf16[1024,7168]{1,0:T(8,128)(2,1)S(1)} %copy-done.1), custom_call_target="tpu_custom_call" | custom-call | tf_op jit(solution)/shard_map/project/pallas_call | solution.py:147
  62.4 6.3 %all-to-all-start.1 = ((bf16[8,16,7168]{2,1,0:T(8,128)(2,1)}), bf16[8,16,7168]{2,1,0:T(8,128)(2,1)S(1)}, u32[]{:S(2)}, u32[]{:S(2)}) async-start(bf16[8,16,7168]{2,1,0:T(8,128)(2,1)} %bitcast.1), calls=%async_computation.1 | async-start | bytes 3670016 | tf_op jit(solution)/shard_map/all_to_all | solution.py:203
  68.6 0.0 copy-done.6
  68.7 22.3 %all-to-all-done.1.partial_ref = bf16[8,16,7168]{2,1,0:T(8,128)(2,1)S(1)} async-done(((bf16[8,16,7168]{2,1,0:T(8,128)(2,1)}), bf16[8,16,7168]{2,1,0:T(8,128)(2,1)S(1)}, u32[]{:S(2)}, u32[]{:S(2)}) %all-to-all-start.1) | async-done | bytes 1835040 | tf_op jit(solution)/shard_map/all_to_all | solution.py:203
  90.9 0.0 copy-done.4
  90.9 1.1 %finish.1 = (bf16[16,7168]{1,0:T(8,128)(2,1)}, bf16[16,7168]{1,0:T(8,128)(2,1)}) custom-call(bf16[8,16,7168]{2,1,0:T(8,128)(2,1)S(1)} %all-to-all-done.1.partial_ref, bf16[16,7168]{1,0:T(8,128)(2,1)S(1)} %copy-done.4, bf16[1,7168]{1,0:T(2,128)(2,1)S(1)} %reshape.15.gain_ref), custom_call_target="tpu_custom_call" | custom-call | tf_op jit(solution)/shard_map/finish/pallas_call | solution.py:179
  (1 shorter events, 0.0 us)
Async XLA Ops:
  0.6 14.3 %copy-start.7 = (s32[128]{0:T(128)S(1)}, s32[128]{0:T(128)}, u32[]{:S(2)}) copy-start(s32[128]{0:T(128)} %param.11) | copy-start | bytes 1540
  0.6 14.4 %copy-start.2 = (bf16[16,64,576]{2,1,0:T(8,128)(2,1)S(1)}, bf16[16,64,576]{2,1,0:T(8,128)(2,1)}, u32[]{:S(2)}) copy-start(bf16[16,64,576]{2,1,0:T(8,128)(2,1)} %queries_ref.1) | copy-start | bytes 3538948
  0.7 14.4 %copy-start.5 = (bf16[16,576]{1,0:T(8,128)(2,1)S(1)}, bf16[16,576]{1,0:T(8,128)(2,1)}, u32[]{:S(2)}) copy-start(bf16[16,576]{1,0:T(8,128)(2,1)} %latent_ref.1) | copy-start | bytes 55300
  0.7 50.5 %copy-start.3 = (bf16[8,512,128]{2,1,0:T(8,128)(2,1)S(1)}, bf16[8,512,128]{2,1,0:T(8,128)(2,1)}, u32[]{:S(2)}) copy-start(bf16[8,512,128]{2,1,0:T(8,128)(2,1)} %value_up_ref.1) | copy-start | bytes 3145732
  15.0 4.0 %copy-start = (bf16[16,512,576]{2,1,0:T(8,128)(2,1)S(1)}, bf16[16,512,576]{2,1,0:T(8,128)(2,1)}, u32[]{:S(2)}) copy-start(bf16[16,512,576]{2,1,0:T(8,128)(2,1)} %copy.10.cache_ref) | copy-start | bytes 28311556
  51.2 5.2 %copy-start.1 = (bf16[1024,7168]{1,0:T(8,128)(2,1)S(1)}, bf16[1024,7168]{1,0:T(8,128)(2,1)}, u32[]{:S(2)}) copy-start(bf16[1024,7168]{1,0:T(8,128)(2,1)} %proj_ref.1) | copy-start | bytes 44040196
  56.4 12.3 %copy-start.6 = (bf16[7168]{0:T(1024)(128)(2,1)S(1)}, bf16[7168]{0:T(1024)(128)(2,1)}, u32[]{:S(2)}) copy-start(bf16[7168]{0:T(1024)(128)(2,1)} %param.15) | copy-start | bytes 43012
  56.4 34.6 %copy-start.4 = (bf16[16,7168]{1,0:T(8,128)(2,1)S(1)}, bf16[16,7168]{1,0:T(8,128)(2,1)}, u32[]{:S(2)}) copy-start(bf16[16,7168]{1,0:T(8,128)(2,1)} %residual_ref.1) | copy-start | bytes 688132
  62.4 28.6 %all-to-all-start.1 = ((bf16[8,16,7168]{2,1,0:T(8,128)(2,1)}), bf16[8,16,7168]{2,1,0:T(8,128)(2,1)S(1)}, u32[]{:S(2)}, u32[]{:S(2)}) async-start(bf16[8,16,7168]{2,1,0:T(8,128)(2,1)} %bitcast.1), calls=%async_computation.1 | async-start | bytes 3670016 | tf_op jit(solution)/shard_map/all_to_all | solution.py:203
